TPU v7x, 32 devices: a whole 2x2x4 slice. The times are simulated.
32 devices in a mesh: blk: 8 (over y, x, core), rep: 4 (over z).
Axes of the slice: x: 2, y: 2, z: 4, core: 2. Of those that a mesh axis runs over, the one named last changes fastest.
Arguments:
- features: bfloat16 [8192, 128], P(('blk', 'rep')), may hold values from -6 to 6
- edge_rows: int32 [8, 8, 8, 512], P('blk', None, 'rep'), may hold values from 0 to 1023
- edge_cols: int32 [8, 8, 8, 512], P('blk', None, 'rep'), may hold values from 0 to 127
- weight: bfloat16 [128, 256], replicated, may hold values from -0.5 to 0.5
- bias: float32 [256], replicated, may hold values from -3 to 3
- upstream: bfloat16 [8192, 256], P('blk'), may hold values from -6 to 6
- train_mask: int32 [8192], P('blk'), may hold values 0 or 1
Outputs:
- activations: bfloat16 [8192, 256], P(('blk', 'rep'))
- grad_features: bfloat16 [8192, 128], P(('blk', 'rep'))
- grad_weight: float32 [128, 256], replicated
- grad_bias: float32 [256], replicated
Inputs may be any that keep to these rules, and one draw needn't show every extreme that they name: `edge_rows`: target indices within a panel. `edge_cols`: source indices within a column block.
All inputs are finite; a program needn't handle non-finite values. No bound on the sum of `train_mask` on one device may be relied on, other than what follows from the above.
Results may differ from a plain program's by a relative error of at most 0.018.
Values may be sent and summed in bfloat16 or wider, within the bound.
A program may use at most 64 MiB of HBM per device.

v0:
```python
import jax
import jax.numpy as jnp
from jax import lax
from jax.sharding import PartitionSpec as P

CB = 128


def dense_layer(feats, gathered, counts, upstream, train_mask, weight, bias):
    degree = 1.0 + counts
    mixed_in = ((feats + gathered) / degree[:, None]).astype(jnp.bfloat16)
    pre_act = jnp.dot(mixed_in, weight, preferred_element_type=jnp.float32) + bias
    gate_value = jax.nn.sigmoid(pre_act)
    activations = (pre_act * gate_value).astype(jnp.bfloat16)
    slope = gate_value * (1.0 + pre_act * (1.0 - gate_value))
    grad_pre = (
        upstream.astype(jnp.float32) * train_mask.astype(jnp.float32)[:, None] * slope
    ).astype(jnp.bfloat16)
    scaled_back = (
        jnp.dot(grad_pre, weight.T, preferred_element_type=jnp.float32) / degree[:, None]
    ).astype(jnp.bfloat16)
    return (mixed_in, activations, grad_pre, scaled_back)


def on_device(features, edge_rows, edge_cols, weight, bias, upstream, train_mask):
    piece_rows, feature_width = features.shape
    edge_slots = edge_rows.shape[-1]
    panel_rows = upstream.shape[0]
    flat_rows = edge_rows.reshape(-1, edge_slots)
    flat_cols = edge_cols.reshape(-1, edge_slots)
    rep_index = lax.axis_index("rep")
    counts_part = jnp.zeros((panel_rows,), jnp.float32).at[flat_rows.reshape(-1)].add(1.0)
    shard_rows = lax.all_gather(features, "blk", axis=0, tiled=True)
    block_count = shard_rows.shape[0] // CB
    offsets = (jnp.arange(block_count, dtype=jnp.int32) * CB)[:, None]
    values = jnp.take(shard_rows, (offsets + flat_cols).reshape(-1), axis=0).astype(jnp.float32)
    partial_sums = (
        jnp.zeros((panel_rows, feature_width), jnp.float32).at[flat_rows.reshape(-1)].add(values)
    )
    placed = lax.dynamic_update_slice_in_dim(
        jnp.zeros((panel_rows, feature_width), jnp.float32),
        features.astype(jnp.float32),
        rep_index * piece_rows,
        0,
    )
    gathered, counts, panel_feats = (
        lax.psum(partial_sums.astype(jnp.bfloat16), "rep").astype(jnp.float32),
        lax.psum(counts_part.astype(jnp.bfloat16), "rep").astype(jnp.float32),
        lax.psum(placed.astype(jnp.bfloat16), "rep").astype(jnp.float32),
    )
    mixed_panel, act_panel, grad_panel, back_panel = dense_layer(
        panel_feats, gathered, counts, upstream, train_mask, weight, bias
    )
    mixed_own = lax.dynamic_slice_in_dim(mixed_panel, rep_index * piece_rows, piece_rows, 0)
    activations = lax.dynamic_slice_in_dim(act_panel, rep_index * piece_rows, piece_rows, 0)
    grad_own = lax.dynamic_slice_in_dim(grad_panel, rep_index * piece_rows, piece_rows, 0)
    back_own = lax.dynamic_slice_in_dim(back_panel, rep_index * piece_rows, piece_rows, 0)
    weight_part = lax.dot_general(
        mixed_own, grad_own, (((0,), (0,)), ((), ())), preferred_element_type=jnp.float32
    )
    bias_part = jnp.sum(grad_own.astype(jnp.float32), axis=0)
    grad_weight, grad_bias = lax.psum((weight_part, bias_part), ("blk", "rep"))
    edge_back = jnp.take(back_panel, edge_rows.reshape(-1), axis=0).reshape(
        edge_rows.shape + (feature_width,)
    )
    moved_back, moved_cols = (
        lax.all_to_all(edge_back, "blk", split_axis=1, concat_axis=0, tiled=True),
        lax.all_to_all(edge_cols, "blk", split_axis=1, concat_axis=0, tiled=True),
    )
    moved_back = moved_back[:, 0]
    moved_cols = moved_cols[:, 0]
    one_hot = (moved_cols[..., None] == jnp.arange(CB, dtype=jnp.int32)).astype(jnp.bfloat16)
    received = jnp.einsum(
        "bnec,bned->ncd", one_hot, moved_back, preferred_element_type=jnp.float32
    ).reshape(piece_rows, feature_width)
    grad_features = (back_own.astype(jnp.float32) + received).astype(jnp.bfloat16)
    return (activations, grad_features, grad_weight, grad_bias)


def solution(mesh):
    return jax.shard_map(
        on_device,
        mesh=mesh,
        in_specs=(
            P(("blk", "rep"), None),
            P("blk", None, "rep", None),
            P("blk", None, "rep", None),
            P(),
            P(),
            P("blk", None),
            P("blk"),
        ),
        out_specs=(P(("blk", "rep"), None), P(("blk", "rep"), None), P(), P()),
        check_vma=False,
    )
```

profile of v0, /device:TPU:0, one launch (start us, length us, event | category | flops | bytes accessed | tf_op | source)
XLA Modules:
  0.0 343.2 jit_solution(15045154229733908388)
XLA Ops:
  7.2 0.0 copy-start
  7.2 0.0 copy-start.2
  7.2 5.3 %all-to-all-start = ((s32[1,8,2,512]{3,2,0,1:T(2,128)}), s32[1,8,2,512]{3,2,0,1:T(2,128)S(1)}, u32[]{:S(2)}, u32[]{:S(2)}) async-start(s32[1,8,2,512]{3,2,0,1:T(2,128)} %bitcast.34), calls=%async_computation | async-start | bytes 65536 | tf_op jit(solution)/shard_map/all_to_all | solution.py:68
  12.5 0.0 all-reduce.6.cloned.1.call-start
  12.6 0.8 reshape.123
  13.4 0.0 copy-start.4
  13.4 0.0 copy-start.3
  13.4 0.8 copy.22
  14.2 0.8 reshape_reshape.6
  15.1 0.1 broadcast_bitcast_fusion
  15.2 0.1 compare_select_fusion
  15.3 10.6 %all_gather.3 = bf16[2048,128]{1,0:T(8,128)(2,1)S(1)} all-gather(bf16[256,128]{1,0:T(8,128)(2,1)} %param.7), channel_id=1, replica_groups=mesh['blk'=8,'rep'=4] {'blk'}, dimensions={0}, use_global_device_ids=true | all-gather | bytes 589824 | tf_op jit(solution)/shard_map/all_gather | solution.py:33
  25.9 0.0 copy-start.5
  25.9 0.0 copy-start.6
  25.9 73.5 %scatter_custom_fusion = f32[1024,128]{1,0:T(8,128)S(1)} fusion(s32[8192]{0:T(1024)S(1)} %bitcast.39, pred[8192]{0:T(1024)(128)(4,1)S(1)} %compare_and_fusion.1, bf16[]{:T(256)} %constant.27.clone.1, f32[]{:T(128)} %constant.13.clone.1, bf16[2048,128]{1,0:T(8,128)(2,1)S(1)} %all_gather.3, s32[8192]{0:T(1024)S(1)} %broadcast_clamp_fusion.1), kind=kCustom, calls=%fused_computation.5 | custom fusion | flops 3145728 | bytes 1089542 | tf_op jit(solution)/shard_map/scatter-add | solution.py:38
  99.4 0.7 convert_element_type.56
  100.1 0.0 copy-done.2
  100.1 0.0 copy-start.1
  100.2 0.7 copy-done.1
  100.9 0.0 all-reduce.6.cloned.1.call-update
  100.9 57.0 %scatter_custom_fusion.1 = f32[1024]{0:T(1024)S(1)} fusion(s32[8192]{0:T(1024)S(1)} %bitcast.40, f32[8192]{0:T(1024)S(1)} %broadcast.105, f32[]{:T(128)} %constant.13.clone.1), kind=kCustom, calls=%fused_computation.42 | custom fusion | flops 8192 | bytes 4100 | tf_op jit(solution)/shard_map/scatter-add | solution.py:32
  157.9 12.0 %psum.37 = bf16[1024]{0:T(1024)(128)(2,1)S(1)} all-reduce(bf16[1024]{0:T(1024)(128)(2,1)S(1)} %convert_element_type.58), channel_id=1, replica_groups=mesh['blk'=8,'rep'=4] {'rep'}, use_global_device_ids=true, to_apply=%region_4.5 | all-reduce | flops 1024 | bytes 4096 | tf_op jit(solution)/shard_map/psum | solution.py:48
  169.9 0.0 copy-done.4
  169.9 0.0 copy-done.3
  170.0 0.0 all-reduce.6.cloned.1.call-done
  170.0 1.2 divide_convert_fusion
  171.3 0.0 copy-done
  171.3 0.0 copy-done.5
  171.3 0.0 copy-done.6
  171.3 1.9 multiply_convert_fusion
  173.2 0.3 fusion.8
  173.5 24.0 %gather_fusion = bf16[8192,128]{1,0:T(8,128)(2,1)S(1)} fusion(bf16[1024,128]{1,0:T(8,128)(2,1)S(1)} %fusion.8, s32[8192]{0:T(1024)S(1)} %broadcast_clamp_fusion), kind=kCustom, calls=%fused_computation.1 | custom fusion | bytes 4227072 | tf_op jit(solution)/shard_map/jit(_take)/gather | solution.py:63
  197.5 2.7 select_bitcast_fusion
  200.2 0.0 all-to-all-done
  200.2 3.6 %all-to-all-start.1 = ((bf16[1,8,2,512,128]{4,3,2,0,1:T(8,128)(2,1)}), bf16[1,8,2,512,128]{4,3,2,0,1:T(8,128)(2,1)S(1)}, u32[]{:S(2)}, u32[]{:S(2)}) async-start(bf16[1,8,2,512,128]{4,3,2,0,1:T(8,128)(2,1)} %select_bitcast_fusion), calls=%async_computation.1 | async-start | bytes 4194304 | tf_op jit(solution)/shard_map/all_to_all | solution.py:67
  203.8 0.0 all-reduce.4.cloned.1.call-start
  203.9 0.9 fusion.13
  204.7 0.0 all-reduce.4.cloned.1.call-update
  204.8 0.1 convert_reduce_fusion
  204.8 57.2 %psum.39 = f32[256]{0:T(256)} all-reduce(f32[256]{0:T(256)S(1)} %convert_reduce_fusion), channel_id=1, replica_groups=mesh['blk'=8,'rep'=4] {'blk','rep'}, use_global_device_ids=true, to_apply=%region_7.8 | all-reduce | flops 256 | bytes 2048 | tf_op jit(solution)/shard_map/psum | solution.py:62
  262.0 1.7 fusion.10
  263.7 0.0 all-to-all-done.1
  263.7 0.9 fusion.2
  264.6 0.7 fusion.12
  265.3 69.5 %all-reduce.4.cloned.1.call-done = f32[128,256]{1,0:T(8,128)} async-done(((f32[128,256]{1,0:T(8,128)}), f32[128,256]{1,0:T(8,128)}) %all-reduce.4.cloned.1.call-update) | async-done | bytes 131088 | tf_op jit(solution)/shard_map/psum | solution.py:62
  334.8 1.6 copy.32
  (15 shorter events, 0.2 us)
Async XLA Ops:
  7.2 164.1 %copy-start = (bf16[128,256]{1,0:T(8,128)(2,1)S(1)}, bf16[128,256]{1,0:T(8,128)(2,1)}, u32[]{:S(2)}) copy-start(bf16[128,256]{1,0:T(8,128)(2,1)} %param.10) | copy-start | bytes 196612
  7.2 92.9 %copy-start.2 = (bf16[256,128]{1,0:T(8,128)(2,1)S(1)}, bf16[256,128]{1,0:T(8,128)(2,1)}, u32[]{:S(2)}) copy-start(bf16[256,128]{1,0:T(8,128)(2,1)} %param.7) | copy-start | bytes 196612
  7.2 193.0 %all-to-all-start = ((s32[1,8,2,512]{3,2,0,1:T(2,128)}), s32[1,8,2,512]{3,2,0,1:T(2,128)S(1)}, u32[]{:S(2)}, u32[]{:S(2)}) async-start(s32[1,8,2,512]{3,2,0,1:T(2,128)} %bitcast.34), calls=%async_computation | async-start | bytes 65536 | tf_op jit(solution)/shard_map/all_to_all | solution.py:68
  12.5 157.5 %all-reduce.6.cloned.1.call-start = ((), (), s32[]{:S(2)}) async-start(), calls=%async_computation.3 | async-start | bytes 1048576 | tf_op jit(solution)/shard_map/psum | solution.py:47
  13.4 156.5 %copy-start.4 = (s32[1024]{0:T(1024)S(1)}, s32[1024]{0:T(1024)}, u32[]{:S(2)}) copy-start(s32[1024]{0:T(1024)} %param.13) | copy-start | bytes 12292
  13.4 156.5 %copy-start.3 = (s32[1,8,2,512]{3,2,1,0:T(2,128)S(1)}, s32[1,8,2,512]{3,2,1,0:T(2,128)}, u32[]{:S(2)}) copy-start(s32[1,8,2,512]{3,2,1,0:T(2,128)} %param.8) | copy-start | bytes 98308
  25.9 145.4 %copy-start.5 = (bf16[1024,256]{1,0:T(8,128)(2,1)S(1)}, bf16[1024,256]{1,0:T(8,128)(2,1)}, u32[]{:S(2)}) copy-start(bf16[1024,256]{1,0:T(8,128)(2,1)} %param.12) | copy-start | bytes 1572868
  25.9 145.4 %copy-start.6 = (f32[256]{0:T(256)S(1)}, f32[256]{0:T(256)}, u32[]{:S(2)}) copy-start(f32[256]{0:T(256)} %param.11) | copy-start | bytes 3076
  100.1 0.7 copy-start.1
  200.2 63.5 %all-to-all-start.1 = ((bf16[1,8,2,512,128]{4,3,2,0,1:T(8,128)(2,1)}), bf16[1,8,2,512,128]{4,3,2,0,1:T(8,128)(2,1)S(1)}, u32[]{:S(2)}, u32[]{:S(2)}) async-start(bf16[1,8,2,512,128]{4,3,2,0,1:T(8,128)(2,1)} %select_bitcast_fusion), calls=%async_computation.1 | async-start | bytes 4194304 | tf_op jit(solution)/shard_map/all_to_all | solution.py:67
  203.8 131.0 %all-reduce.4.cloned.1.call-start = ((), (), s32[]{:S(2)}) async-start(), calls=%async_computation.2 | async-start | bytes 262144 | tf_op jit(solution)/shard_map/psum | solution.py:62
Sparse Core Ops, SparseCore 0:
  101.0 38.8 all-reduce.5
  210.8 123.9 all-reduce.3
where the time goes:
time: 344 us; the launch traced here: 343 us
  other arithmetic  138 us (40%)
  blocking collectives  79.8 us (23%)
  waiting for transfers between devices  69.6 us (20%)
  local copies, waits for them, and re-layouts  28.9 us (8%)
  between operations  14.3 us (4%)
  starting transfers between devices  9 us (3%)
  matrix products  3.94 us (1%)
    scatter-add x1, other arithmetic, on_device(): jnp.zeros((panel_rows, feature_width), jnp.float32)  73.5 us
    psum x1, waiting for transfers between devices, on_device(): grad_weight, grad_bias = lax.psum((weight_part, bias_part), ('blk', 'rep'))  69.5 us
    psum x1, blocking collectives, on_device(): grad_weight, grad_bias = lax.psum((weight_part, bias_part), ('blk', 'rep'))  57.2 us
    scatter-add x1, other arithmetic, on_device(): jnp.zeros((panel_rows,), jnp.float32).at[flat_rows.reshape(-1)].add(1.0)  57 us
    gather x1, local copies, waits for them, and re-layouts, on_device(): jnp.take(back_panel, edge_rows.reshape(-1), axis=0)  24 us
    psum x1, blocking collectives, on_device(): lax.psum(counts_part.astype(jnp.bfloat16), 'rep').astype(jnp.float32)  12 us
    all_gather x1, blocking collectives, on_device(): shard_rows = lax.all_gather(features, 'blk', axis=0, tiled=True)  10.6 us
  transfers between devices with their start and end apart: 4, of which 1 were waited for; matrix products, arithmetic and copies ran while one was open for 49% of the time, Pallas kernels for 0%

commit v1 on v0

v1 whole, which is shorter than its diff:
```python
import functools

import jax
import jax.numpy as jnp
from jax import lax
from jax.experimental import pallas as pl
from jax.experimental.pallas import tpu as pltpu
from jax.sharding import PartitionSpec as P

CB = 128
F32 = jnp.float32
BF16 = jnp.bfloat16
MESH = pl.DeviceIdType.MESH
NT = (((1,), (1,)), ((), ()))


def column(row):
    return jnp.broadcast_to(row, (CB, CB)).T


def one_hot(index, count):
    length = index.shape[-1]
    spot = lax.broadcasted_iota(jnp.int32, (count, length), 0)
    return jnp.where(spot == index, 1.0, 0.0).astype(BF16)


def kernel(
    n_blk, n_rep, keep,
    feat_ref, rows_ref, cols_ref, weight_ref, bias_ref, mask_ref, up_hbm,
    act_ref, gf_ref, gw_ref, gb_ref,
    fbuf, amat, acc, psend, precv, upbuf, backs, oacc, gsend, grecv,
    w1s, w1r, w2s, w2r, w3s, w3r,
    f_ss, f_rs, p_ss, p_rs, b_ss, b_rs, g_ss, g_rs, w1_ss, w1_rs, w2_ss, w2_rs, w3_ss, w3_rs, up_sem,
):
    b = lax.axis_index("blk")
    z = lax.axis_index("rep")
    piece, d_in = feat_ref.shape
    panel = piece * n_rep
    hid = weight_ref.shape[1]
    chunks = piece // CB
    wch = d_in // n_blk

    def blk_at(k):
        return lax.rem(b + k, n_blk)

    def rep_at(j):
        return lax.rem(z + j, n_rep)

    def send(src, dst, ss, rs, i, **where):
        copy = pltpu.make_async_remote_copy(
            src_ref=src, dst_ref=dst, send_sem=ss.at[i], recv_sem=rs.at[i],
            device_id=where, device_id_type=MESH,
        )
        copy.start()
        return copy

    barrier = pltpu.get_barrier_semaphore()
    for k in range(1, n_blk):
        pl.semaphore_signal(barrier, inc=1, device_id={"blk": blk_at(k)}, device_id_type=MESH)
    for j in range(1, n_rep):
        pl.semaphore_signal(barrier, inc=1, device_id={"rep": rep_at(j)}, device_id_type=MESH)
    up_copy = pltpu.make_async_copy(
        up_hbm.at[pl.ds(pl.multiple_of(z * piece, piece), piece)], upbuf, up_sem
    )
    up_copy.start()
    fbuf[b] = feat_ref[...]
    pl.semaphore_wait(barrier, n_blk + n_rep - 2)

    sent = []
    f_copies = [
        send(feat_ref, fbuf.at[b], f_ss, f_rs, k, blk=blk_at(k)) for k in range(1, n_blk)
    ]
    sent += f_copies

    def build(q, slot):
        for c in range(chunks):
            rows = rows_ref[0, q, pl.ds(c, 1), :]
            cols = cols_ref[0, q, pl.ds(c, 1), :]
            length = rows.shape[-1]
            col_hot = one_hot(cols, CB)
            low_hot = one_hot(rows & (CB - 1), CB)
            high = jnp.broadcast_to(rows >> 7, (16, length))
            parts = []
            for h in range(panel // CB):
                picked = jnp.where(high == h, 1.0, 0.0).astype(BF16)
                parts.append(low_hot * jnp.concatenate([picked] * (CB // 16), axis=0))
            row_hot = jnp.concatenate(parts, axis=0)
            amat[slot, :, c * CB:(c + 1) * CB] = lax.dot_general(
                row_hot, col_hot, NT, preferred_element_type=F32
            ).astype(BF16)

    def with_ones(q):
        return jnp.concatenate([fbuf[q], jnp.ones((piece, CB), BF16)], axis=1)

    def pack(total, slot):
        psend[slot, 0:piece, :] = total[:, :d_in].astype(BF16)
        counts = total[:, d_in:]
        tall = jnp.concatenate(
            [counts[i * CB:(i + 1) * CB].T[0:16] for i in range(chunks)], axis=0
        )
        top = tall.astype(BF16).astype(F32)
        line = lax.broadcasted_iota(jnp.int32, tall.shape, 0)
        psend[slot, piece:, :] = jnp.where(line % 16 < 8, top, tall - top).astype(BF16)

    if keep:
        def build_step(q, carry):
            build(q, q)
            return carry
        lax.fori_loop(0, n_blk, build_step, 0)
        for copy in f_copies:
            copy.wait_recv()
    else:
        for copy in f_copies:
            copy.wait_recv()
        acc[...] = jnp.zeros_like(acc)

        def both_step(q, carry):
            build(q, 0)
            acc[...] += jnp.dot(amat[0], with_ones(q), preferred_element_type=F32)
            return carry
        lax.fori_loop(0, n_blk, both_step, 0)

    p_copies = []
    for j in list(range(1, n_rep)) + [0]:
        at = pl.ds(pl.multiple_of(rep_at(j) * piece, piece), piece)
        if keep:
            def part_step(q, total):
                return total + jnp.dot(amat[q, at, :], with_ones(q), preferred_element_type=F32)
            total = lax.fori_loop(0, n_blk, part_step, jnp.zeros((piece, d_in + CB), F32))
        else:
            total = acc[at, :]
        pack(total, j)
        if j > 0:
            p_copies.append(
                send(psend.at[j], precv.at[j], p_ss, p_rs, j, rep=rep_at(j))
            )
    sent += p_copies

    gathered = psend[0, 0:piece, :].astype(F32)
    tail = psend[0, piece:, :].astype(F32)
    up_copy.wait()
    for copy, j in zip(p_copies, range(1, n_rep)):
        copy.wait_recv()
        gathered = gathered + precv[j, 0:piece, :].astype(F32)
        tail = tail + precv[j, piece:, :].astype(F32)
    degree_rows = [
        1.0 + tail[16 * i:16 * i + 1] + tail[16 * i + 8:16 * i + 9] for i in range(chunks)
    ]
    degree = jnp.concatenate([column(row) for row in degree_rows], axis=0)
    mixed = ((feat_ref[...].astype(F32) + gathered) / degree).astype(BF16)
    pre_act = jnp.dot(mixed, weight_ref[...], preferred_element_type=F32) + bias_ref[...]
    gate = jax.nn.sigmoid(pre_act)
    slope = gate * (1.0 + pre_act * (1.0 - gate))
    mask = jnp.concatenate(
        [column(mask_ref[pl.ds(z * chunks + i, 1), :].astype(F32)) for i in range(chunks)], axis=0
    )
    mask = jnp.concatenate([mask] * (hid // CB), axis=1)
    grad_pre = (upbuf[...].astype(F32) * mask * slope).astype(BF16)
    back = lax.dot_general(weight_ref[...], grad_pre, NT, preferred_element_type=F32)
    backs[0] = (back / jnp.concatenate(degree_rows, axis=1)).astype(BF16)
    b_copies = {
        j: send(backs.at[0], backs.at[j], b_ss, b_rs, j, rep=rep_at(j)) for j in range(1, n_rep)
    }
    sent += list(b_copies.values())

    act_ref[...] = (pre_act * gate).astype(BF16)
    weight_part = jnp.dot(
        mixed.astype(F32).T.astype(BF16), grad_pre, preferred_element_type=F32
    )
    bias_part = jnp.broadcast_to(
        jnp.sum(grad_pre.astype(F32), axis=0, keepdims=True), (8, hid)
    )
    for q in range(n_blk):
        w1s[q, 0:wch, :] = weight_part[q * wch:(q + 1) * wch]
        w1s[q, wch:, :] = bias_part
    w1r[b] = w1s[b]
    w1_copies = [
        send(w1s.at[blk_at(k)], w1r.at[b], w1_ss, w1_rs, k, blk=blk_at(k)) for k in range(1, n_blk)
    ]
    sent += w1_copies

    def reduce_first():
        for copy in w1_copies:
            copy.wait_recv()
        total = w1r[0]
        for q in range(1, n_blk):
            total = total + w1r[q]
        w2s[...] = total
        w2r[z] = total
        copies = [
            send(w2s, w2r.at[z], w2_ss, w2_rs, j, rep=rep_at(j)) for j in range(1, n_rep)
        ]
        return copies

    def reduce_second(copies):
        for copy in copies:
            copy.wait_recv()
        total = w2r[0]
        for q in range(1, n_rep):
            total = total + w2r[q]
        gb_ref[...] = total[wch:wch + 1]
        w3s[...] = total[0:wch]
        w3r[b] = total[0:wch]
        return [
            send(w3s, w3r.at[b], w3_ss, w3_rs, k, blk=blk_at(k)) for k in range(1, n_blk)
        ]

    order = [0] + list(range(1, n_rep))

    def rows_of(j):
        return pl.ds(pl.multiple_of(rep_at(n_rep - j) * piece, piece), piece)

    if keep:
        def first_step(q, carry):
            oacc[q] = jnp.dot(backs[0], amat[q, rows_of(0), :], preferred_element_type=F32)
            return carry
        lax.fori_loop(0, n_blk, first_step, 0)
        for j in order[1:-1]:
            b_copies[j].wait_recv()

            def more_step(q, carry, j=j):
                oacc[q] += jnp.dot(backs[j], amat[q, rows_of(j), :], preferred_element_type=F32)
                return carry
            lax.fori_loop(0, n_blk, more_step, 0)
        b_copies[order[-1]].wait_recv()
    else:
        for j in order[1:]:
            b_copies[j].wait_recv()

        def back_step(q, carry):
            build(q, 0)
            total = jnp.dot(backs[0], amat[0, rows_of(0), :], preferred_element_type=F32)
            for j in order[1:]:
                total = total + jnp.dot(backs[j], amat[0, rows_of(j), :], preferred_element_type=F32)
            oacc[q] = total
            return carry
        lax.fori_loop(0, n_blk, back_step, 0)

    g_copies = []
    for k in list(range(1, n_blk)) + [0]:
        q = blk_at(k)
        total = oacc[q]
        if keep:
            j = order[-1]
            total = total + jnp.dot(backs[j], amat[q, rows_of(j), :], preferred_element_type=F32)
        if k > 0:
            gsend[k] = total.astype(BF16)
            g_copies.append(send(gsend.at[k], grecv.at[k], g_ss, g_rs, k, blk=q))
        else:
            result = total + backs[0].astype(F32)
    sent += g_copies

    w2_copies = reduce_first()
    sent += w2_copies
    w3_copies = reduce_second(w2_copies)
    sent += w3_copies
    for k, copy in zip(range(1, n_blk), g_copies):
        copy.wait_recv()
        result = result + grecv[k].astype(F32)
    gf_ref[...] = result.T.astype(BF16)
    for copy in w3_copies:
        copy.wait_recv()
    for q in range(n_blk):
        gw_ref[q * wch:(q + 1) * wch, :] = w3r[q]
    for copy in sent:
        copy.wait_send()


def on_device(n_blk, n_rep, features, edge_rows, edge_cols, weight, bias, upstream, train_mask):
    piece, d_in = features.shape
    panel = upstream.shape[0]
    hid = weight.shape[1]
    wch = d_in // n_blk
    extra = 16 * (piece // CB)
    keep = panel * piece * n_blk * 2 <= 16 * 2**20
    sem = pltpu.SemaphoreType.DMA
    vmem = pl.BlockSpec(memory_space=pltpu.VMEM)
    act, gf, gw, gb = pl.pallas_call(
        functools.partial(kernel, n_blk, n_rep, keep),
        out_shape=(
            jax.ShapeDtypeStruct((piece, hid), BF16),
            jax.ShapeDtypeStruct((piece, d_in), BF16),
            jax.ShapeDtypeStruct((d_in, hid), F32),
            jax.ShapeDtypeStruct((1, hid), F32),
        ),
        in_specs=[vmem] * 6 + [pl.BlockSpec(memory_space=pl.ANY)],
        out_specs=(vmem,) * 4,
        scratch_shapes=[
            pltpu.VMEM((n_blk, piece, d_in), BF16),
            pltpu.VMEM((n_blk if keep else 1, panel, piece), BF16),
            pltpu.VMEM((8 if keep else panel, d_in + CB), F32),
            pltpu.VMEM((n_rep, piece + extra, d_in), BF16),
            pltpu.VMEM((n_rep, piece + extra, d_in), BF16),
            pltpu.VMEM((piece, hid), BF16),
            pltpu.VMEM((n_rep, d_in, piece), BF16),
            pltpu.VMEM((n_blk, d_in, piece), F32),
            pltpu.VMEM((n_blk, d_in, piece), BF16),
            pltpu.VMEM((n_blk, d_in, piece), BF16),
            pltpu.VMEM((n_blk, wch + 8, hid), F32),
            pltpu.VMEM((n_blk, wch + 8, hid), F32),
            pltpu.VMEM((wch + 8, hid), F32),
            pltpu.VMEM((n_rep, wch + 8, hid), F32),
            pltpu.VMEM((wch, hid), F32),
            pltpu.VMEM((n_blk, wch, hid), F32),
            sem((n_blk,)), sem((n_blk,)),
            sem((n_rep,)), sem((n_rep,)),
            sem((n_rep,)), sem((n_rep,)),
            sem((n_blk,)), sem((n_blk,)),
            sem((n_blk,)), sem((n_blk,)),
            sem((n_rep,)), sem((n_rep,)),
            sem((n_blk,)), sem((n_blk,)),
            sem,
        ],
        compiler_params=pltpu.CompilerParams(
            collective_id=0, has_side_effects=True, vmem_limit_bytes=48 * 2**20
        ),
    )(
        features, edge_rows, edge_cols, weight, bias.reshape(1, hid),
        train_mask.reshape(panel // CB, CB), upstream,
    )
    return act, gf, gw, gb.reshape(hid)


def solution(mesh):
    n_blk, n_rep = mesh.shape["blk"], mesh.shape["rep"]
    return jax.shard_map(
        functools.partial(on_device, n_blk, n_rep),
        mesh=mesh,
        in_specs=(
            P(("blk", "rep"), None),
            P("blk", None, "rep", None),
            P("blk", None, "rep", None),
            P(),
            P(),
            P("blk", None),
            P("blk"),
        ),
        out_specs=(P(("blk", "rep"), None), P(("blk", "rep"), None), P(), P()),
        check_vma=False,
    )
```

time: 344 us -> 52.1 us (0.15)
  other arithmetic: 138 us -> 0 us
  blocking collectives: 79.8 us -> 0 us
  waiting for transfers between devices: 69.6 us -> 0 us
  Pallas kernels: 0 us -> 42.9 us
  local copies, waits for them, and re-layouts: 28.9 us -> 8.1 us
  between operations: 14.3 us -> 0.66 us
  starting transfers between devices: 9 us -> 0 us
  matrix products: 3.94 us -> 0 us
    scatter-add x2 -> x0, other arithmetic: 130 us -> none  [the longest x1 73.5 us: on_device(): jnp.zeros((panel_rows, feature_width), jnp.float32)]
    psum x2 -> x0, waiting for transfers between devices: 69.5 us -> none  [the longest x1 69.5 us: on_device(): grad_weight, grad_bias = lax.psum((weight_part, bias_part), ('blk', 'rep'))]
    psum x2 -> x0, blocking collectives: 69.2 us -> none  [the longest x1 57.2 us: on_device(): grad_weight, grad_bias = lax.psum((weight_part, bias_part), ('blk', 'rep'))]
    pallas_call x0 -> x1, Pallas kernels: none -> 42.9 us  [on_device(): pl.pallas_call(functools.partial(kernel, n_blk, n_rep, keep), out_shape=(...]
    gather x1 -> x0, local copies, waits for them, and re-layouts: 24 us -> none  [on_device(): jnp.take(back_panel, edge_rows.reshape(-1), axis=0)]
    all_gather x1 -> x0, blocking collectives: 10.6 us -> none  [on_device(): shard_rows = lax.all_gather(features, 'blk', axis=0, tiled=True)]
    all_to_all x2 -> x0, starting transfers between devices: 8.92 us -> none  [the longest x1 5.31 us: on_device(): lax.all_to_all(edge_cols, 'blk', split_axis=1, concat_axis=0, tiled=True)]
    unnamed x19 -> x18, local copies, waits for them, and re-layouts: 3.19 us -> 8.1 us
  transfers between devices with their start and end apart: 4 -> 0, of which waited for: 1 -> 0; matrix products, arithmetic and copies ran while one was open for 49% -> 0% of each run, Pallas kernels for 0% -> 0%
where the time goes in v1:
time: 52.1 us; the launch traced here: 51.7 us
  Pallas kernels  42.9 us (82%)
  local copies, waits for them, and re-layouts  8.1 us (16%)
  between operations  0.66 us (1%)
    pallas_call x1, Pallas kernels, on_device(): pl.pallas_call(functools.partial(kernel, n_blk, n_rep, keep), out_shape=(...  42.9 us
    unnamed x18, local copies, waits for them, and re-layouts  8.1 us

profile of v1, /device:TPU:0, one launch (start us, length us, event | category | flops | bytes accessed | tf_op | source)
XLA Modules:
  0.0 51.7 jit_solution(12513353554506841527)
XLA Ops:
  0.6 0.0 copy-start.6
  0.6 0.7 %copy-done.6 = f32[256]{0:T(256)S(1)} copy-done((f32[256]{0:T(256)S(1)}, f32[256]{0:T(256)}, u32[]{:S(2)}) %copy-start.6) | copy-done | bytes 1048
  1.3 0.0 copy-start
  1.3 1.0 %copy-done = bf16[1024,256]{1,0:T(8,128)(2,1)S(1)} copy-done((bf16[1024,256]{1,0:T(8,128)(2,1)S(1)}, bf16[1024,256]{1,0:T(8,128)(2,1)}, u32[]{:S(2)}) %copy-start) | copy-done | bytes 524312
  2.4 0.0 copy-start.1
  2.4 0.8 %copy-done.1 = bf16[256,128]{1,0:T(8,128)(2,1)S(1)} copy-done((bf16[256,128]{1,0:T(8,128)(2,1)S(1)}, bf16[256,128]{1,0:T(8,128)(2,1)}, u32[]{:S(2)}) %copy-start.1) | copy-done | bytes 65560
  3.2 0.0 copy-start.2
  3.2 0.8 %copy-done.2 = bf16[128,256]{1,0:T(8,128)(2,1)S(1)} copy-done((bf16[128,256]{1,0:T(8,128)(2,1)S(1)}, bf16[128,256]{1,0:T(8,128)(2,1)}, u32[]{:S(2)}) %copy-start.2) | copy-done | bytes 65560
  4.0 0.0 copy-start.3
  4.0 0.8 %copy-done.3 = s32[1,8,2,512]{3,2,1,0:T(2,128)S(1)} copy-done((s32[1,8,2,512]{3,2,1,0:T(2,128)S(1)}, s32[1,8,2,512]{3,2,1,0:T(2,128)}, u32[]{:S(2)}) %copy-start.3) | copy-done | bytes 32792
  4.8 0.0 copy-start.4
  4.8 0.8 %copy-done.4 = s32[1,8,2,512]{3,2,1,0:T(2,128)S(1)} copy-done((s32[1,8,2,512]{3,2,1,0:T(2,128)S(1)}, s32[1,8,2,512]{3,2,1,0:T(2,128)}, u32[]{:S(2)}) %copy-start.4) | copy-done | bytes 32792
  5.6 0.0 copy-start.5
  5.6 0.7 %copy-done.5 = s32[1024]{0:T(1024)S(1)} copy-done((s32[1024]{0:T(1024)S(1)}, s32[1024]{0:T(1024)}, u32[]{:S(2)}) %copy-start.5) | copy-done | bytes 4120
  6.2 42.9 %shard_map.102 = (bf16[256,256]{1,0:T(8,128)(2,1)S(1)}, bf16[256,128]{1,0:T(8,128)(2,1)S(1)}, f32[128,256]{1,0:T(8,128)S(1)}, f32[1,256]{1,0:T(1,128)S(1)}) custom-call(bf16[256,128]{1,0:T(8,128)(2,1)S(1)} %copy-done.1, s32[1,8,2,512]{3,2,1,0:T(2,128)S(1)} %copy-done.3, s32[1,8,2,512]{3,2,1,0:T(2,128)S(1)} %copy-done.4, bf16[128,256]{1,0:T(8,128)(2,1)S(1)} %copy-done.2, ...), custom_call_target="tpu_custom_call" | custom-call | tf_op jit(solution)/shard_map/pallas_call | solution.py:278
  49.2 0.7 %copy.15 = bf16[256,256]{1,0:T(8,128)(2,1)} copy(bf16[256,256]{1,0:T(8,128)(2,1)S(1)} %get-tuple-element.16) | data formatting | bytes 262144
  49.8 0.6 %copy.16 = bf16[256,128]{1,0:T(8,128)(2,1)} copy(bf16[256,128]{1,0:T(8,128)(2,1)S(1)} %get-tuple-element.17) | data formatting | bytes 131072
  50.5 0.7 %copy.17 = f32[128,256]{1,0:T(8,128)} copy(f32[128,256]{1,0:T(8,128)S(1)} %get-tuple-element.18) | data formatting | bytes 262144
  51.1 0.6 %copy.18 = f32[256]{0:T(256)} copy(f32[256]{0:T(256)S(1)} %bitcast.5) | data formatting | bytes 2048
Async XLA Ops:
  0.6 0.7 %copy-start.6 = (f32[256]{0:T(256)S(1)}, f32[256]{0:T(256)}, u32[]{:S(2)}) copy-start(f32[256]{0:T(256)} %param.11) | copy-start | bytes 3076
  1.3 1.0 %copy-start = (bf16[1024,256]{1,0:T(8,128)(2,1)S(1)}, bf16[1024,256]{1,0:T(8,128)(2,1)}, u32[]{:S(2)}) copy-start(bf16[1024,256]{1,0:T(8,128)(2,1)} %up_hbm.1) | copy-start | bytes 1572868
  2.4 0.8 %copy-start.1 = (bf16[256,128]{1,0:T(8,128)(2,1)S(1)}, bf16[256,128]{1,0:T(8,128)(2,1)}, u32[]{:S(2)}) copy-start(bf16[256,128]{1,0:T(8,128)(2,1)} %feat_ref.1) | copy-start | bytes 196612
  3.2 0.8 %copy-start.2 = (bf16[128,256]{1,0:T(8,128)(2,1)S(1)}, bf16[128,256]{1,0:T(8,128)(2,1)}, u32[]{:S(2)}) copy-start(bf16[128,256]{1,0:T(8,128)(2,1)} %weight_ref.1) | copy-start | bytes 196612
  4.0 0.8 %copy-start.3 = (s32[1,8,2,512]{3,2,1,0:T(2,128)S(1)}, s32[1,8,2,512]{3,2,1,0:T(2,128)}, u32[]{:S(2)}) copy-start(s32[1,8,2,512]{3,2,1,0:T(2,128)} %rows_ref.1) | copy-start | bytes 98308
  4.8 0.8 %copy-start.4 = (s32[1,8,2,512]{3,2,1,0:T(2,128)S(1)}, s32[1,8,2,512]{3,2,1,0:T(2,128)}, u32[]{:S(2)}) copy-start(s32[1,8,2,512]{3,2,1,0:T(2,128)} %cols_ref.1) | copy-start | bytes 98308
  5.6 0.7 %copy-start.5 = (s32[1024]{0:T(1024)S(1)}, s32[1024]{0:T(1024)}, u32[]{:S(2)}) copy-start(s32[1024]{0:T(1024)} %param.13) | copy-start | bytes 12292

commit v2 on v1

v2 whole, which is shorter than its diff:
```python
import functools

import jax
import jax.numpy as jnp
from jax import lax
from jax.experimental import pallas as pl
from jax.experimental.pallas import tpu as pltpu
from jax.sharding import PartitionSpec as P

CB = 128
VMEM = 63 * 2**20
F32 = jnp.float32
BF16 = jnp.bfloat16
MESH = pl.DeviceIdType.MESH
NT = (((1,), (1,)), ((), ()))


def column(row):
    return jnp.broadcast_to(row, (CB, CB)).T


def partner(me, k, count):
    other, bit = 0, 1
    while bit < count:
        other += lax.rem(lax.div(me, bit) + (k // bit) % 2, 2) * bit
        bit *= 2
    return other


def one_hot(index, count):
    length = index.shape[-1]
    spot = lax.broadcasted_iota(jnp.int32, (count, length), 0)
    return jnp.where(spot == index, 1.0, 0.0).astype(BF16)


def kernel(
    n_blk, n_rep, keep,
    feat_hbm, rows_hbm, cols_hbm, weight_hbm, bias_hbm, mask_hbm, up_hbm,
    act_hbm, gf_hbm, gw_hbm, gb_hbm,
    feat_ref, rows_ref, cols_ref, weight_ref, bias_ref, mask_ref,
    act_ref, gf_ref, gw_ref, gb_ref, lowh, colh, fbuf, amat, acc, psend, precv, upbuf, backs, oacc, gsend, grecv,
    w1s, w1r, w2s, w2r, w3s, w3r,
    f_ss, f_rs, p_ss, p_rs, b_ss, b_rs, g_ss, g_rs, w1_ss, w1_rs, w2_ss, w2_rs, w3_ss, w3_rs, in_sem, out_sem,
):
    b = lax.axis_index("blk")
    z = lax.axis_index("rep")
    piece, d_in = feat_ref.shape
    panel = piece * n_rep
    hid = weight_ref.shape[1]
    chunks = piece // CB
    wch = d_in // n_blk

    def blk_at(k):
        return partner(b, k, n_blk)

    def rep_at(j):
        return partner(z, j, n_rep)

    def send(src, dst, ss, rs, i, **where):
        copy = pltpu.make_async_remote_copy(
            src_ref=src, dst_ref=dst, send_sem=ss.at[i], recv_sem=rs.at[i],
            device_id=where, device_id_type=MESH,
        )
        copy.start()
        return copy

    up_src = up_hbm.at[pl.ds(pl.multiple_of(z * piece, piece), piece)]
    loads = [
        pltpu.make_async_copy(src, dst, in_sem.at[i])
        for i, (src, dst) in enumerate((
            (feat_hbm, feat_ref), (rows_hbm, rows_ref), (cols_hbm, cols_ref),
            (weight_hbm, weight_ref), (bias_hbm, bias_ref), (mask_hbm, mask_ref), (up_src, upbuf),
        ))
    ]
    for load in loads:
        load.start()
    barrier = pltpu.get_barrier_semaphore()
    for k in range(1, n_blk):
        pl.semaphore_signal(barrier, inc=1, device_id={"blk": blk_at(k)}, device_id_type=MESH)
    for j in range(1, n_rep):
        pl.semaphore_signal(barrier, inc=1, device_id={"rep": rep_at(j)}, device_id_type=MESH)
    loads[0].wait()
    pl.semaphore_wait(barrier, n_blk + n_rep - 2)

    sent = []
    stored = []

    def store(src, dst):
        copy = pltpu.make_async_copy(src, dst, out_sem.at[len(stored)])
        copy.start()
        stored.append(copy)

    f_copies = [
        send(feat_ref, fbuf.at[b], f_ss, f_rs, k, blk=blk_at(k))
        for k in range(n_blk - 1, 0, -1)
    ]
    sent += f_copies
    fbuf[b] = feat_ref[...]
    for load in loads[1:3]:
        load.wait()

    def prepare(q, slot):
        for c in range(chunks):
            colh[slot, c] = one_hot(cols_ref[0, q, pl.ds(c, 1), :], CB)
            lowh[slot, c] = one_hot(rows_ref[0, q, pl.ds(c, 1), :] & (CB - 1), CB)

    def build(q, slot, first, count):
        made = []
        for c in range(chunks):
            rows = rows_ref[0, q, pl.ds(c, 1), :]
            high = jnp.broadcast_to(rows >> 7, (16, rows.shape[-1]))
            low_hot = lowh[slot, c]
            parts = []
            for h in range(count):
                picked = jnp.where(high == first + h, 1.0, 0.0).astype(BF16)
                parts.append(low_hot * jnp.concatenate([picked] * (CB // 16), axis=0))
            made.append(lax.dot_general(
                jnp.concatenate(parts, axis=0), colh[slot, c], NT, preferred_element_type=F32
            ).astype(BF16))
        at = pl.ds(pl.multiple_of(first * CB, CB), count * CB)
        made = jnp.concatenate(made, axis=1)
        amat[slot, at, :] = made
        return made

    def with_ones(q):
        return jnp.concatenate([fbuf[q], jnp.ones((piece, CB), BF16)], axis=1)

    def pack(total, slot):
        psend[slot, 0:piece, :] = total[:, :d_in].astype(BF16)
        counts = total[:, d_in:]
        tall = jnp.concatenate(
            [counts[i * CB:(i + 1) * CB].T[0:16] for i in range(chunks)], axis=0
        )
        top = tall.astype(BF16).astype(F32)
        line = lax.broadcasted_iota(jnp.int32, tall.shape, 0)
        psend[slot, piece:, :] = jnp.where(line % 16 < 8, top, tall - top).astype(BF16)

    order = ([2, 3] if n_rep == 4 else []) + [j for j in range(1, n_rep) if n_rep != 4 or j == 1]
    p_copies = []

    def piece_of(j):
        return pl.ds(pl.multiple_of(rep_at(j) * piece, piece), piece)

    def push(total, j):
        pack(total, j)
        if j > 0:
            p_copies.append(send(psend.at[j], precv.at[j], p_ss, p_rs, j, rep=rep_at(j)))

    blank = jnp.zeros((piece, d_in + CB), F32)
    if keep:
        def prepare_step(q, carry):
            prepare(q, q)
            return carry
        lax.fori_loop(0, n_blk, prepare_step, 0, unroll=2)
        lead = order[:2]
        for j in lead:
            def build_step(q, carry, j=j):
                build(q, q, rep_at(j) * chunks, chunks)
                return carry
            lax.fori_loop(0, n_blk, build_step, 0, unroll=4)
        for copy in f_copies:
            copy.wait_recv()
        for j in lead:
            def part_step(q, total, j=j):
                return total + jnp.dot(
                    amat[q, piece_of(j), :], with_ones(q), preferred_element_type=F32
                )
            push(lax.fori_loop(0, n_blk, part_step, blank, unroll=4), j)
        for j in order[2:] + [0]:
            def both_step(q, total, j=j):
                made = build(q, q, rep_at(j) * chunks, chunks)
                return total + jnp.dot(made, with_ones(q), preferred_element_type=F32)
            push(lax.fori_loop(0, n_blk, both_step, blank, unroll=4), j)
    else:
        for copy in f_copies:
            copy.wait_recv()
        acc[...] = jnp.zeros_like(acc)

        def whole_step(q, carry):
            prepare(q, 0)
            made = build(q, 0, 0, panel // CB)
            acc[...] += jnp.dot(made, with_ones(q), preferred_element_type=F32)
            return carry
        lax.fori_loop(0, n_blk, whole_step, 0)
        for j in order + [0]:
            push(acc[piece_of(j), :], j)
    sent += p_copies

    gathered = psend[0, 0:piece, :].astype(F32)
    tail = psend[0, piece:, :].astype(F32)
    for load in loads[3:]:
        load.wait()
    for copy, j in zip(p_copies, order):
        copy.wait_recv()
        gathered = gathered + precv[j, 0:piece, :].astype(F32)
        tail = tail + precv[j, piece:, :].astype(F32)
    degree_rows = [
        1.0 + tail[16 * i:16 * i + 1] + tail[16 * i + 8:16 * i + 9] for i in range(chunks)
    ]
    degree = jnp.concatenate([column(row) for row in degree_rows], axis=0)
    mixed = ((feat_ref[...].astype(F32) + gathered) / degree).astype(BF16)
    pre_act = jnp.dot(mixed, weight_ref[...], preferred_element_type=F32) + bias_ref[...]
    gate = jax.nn.sigmoid(pre_act)
    slope = gate * (1.0 + pre_act * (1.0 - gate))
    mask = jnp.concatenate(
        [column(mask_ref[pl.ds(z * chunks + i, 1), :].astype(F32)) for i in range(chunks)], axis=0
    )
    mask = jnp.concatenate([mask] * (hid // CB), axis=1)
    grad_pre = (upbuf[...].astype(F32) * mask * slope).astype(BF16)
    back = lax.dot_general(weight_ref[...], grad_pre, NT, preferred_element_type=F32)
    backs[0] = (back / jnp.concatenate(degree_rows, axis=1)).astype(BF16)
    b_copies = {
        j: send(backs.at[0], backs.at[j], b_ss, b_rs, j, rep=rep_at(j)) for j in order
    }
    sent += list(b_copies.values())

    act_ref[...] = (pre_act * gate).astype(BF16)
    store(act_ref, act_hbm)
    weight_part = jnp.dot(
        mixed.astype(F32).T.astype(BF16), grad_pre, preferred_element_type=F32
    )
    bias_part = jnp.broadcast_to(
        jnp.sum(grad_pre.astype(F32), axis=0, keepdims=True), (8, hid)
    )
    for q in range(n_blk):
        w1s[q, 0:wch, :] = weight_part[q * wch:(q + 1) * wch]
        w1s[q, wch:, :] = bias_part
    w1r[b] = w1s[b]
    w1_copies = [
        send(w1s.at[blk_at(k)], w1r.at[b], w1_ss, w1_rs, k, blk=blk_at(k)) for k in range(1, n_blk)
    ]
    sent += w1_copies

    def reduce_first():
        for copy in w1_copies:
            copy.wait_recv()
        total = w1r[0]
        for q in range(1, n_blk):
            total = total + w1r[q]
        w2s[...] = total
        w2r[z] = total
        copies = [
            send(w2s, w2r.at[z], w2_ss, w2_rs, j, rep=rep_at(j)) for j in range(1, n_rep)
        ]
        return copies

    def reduce_second(copies):
        for copy in copies:
            copy.wait_recv()
        total = w2r[0]
        for q in range(1, n_rep):
            total = total + w2r[q]
        gb_ref[...] = total[wch:wch + 1]
        store(gb_ref, gb_hbm)
        w3s[...] = total[0:wch]
        w3r[b] = total[0:wch]
        return [
            send(w3s, w3r.at[b], w3_ss, w3_rs, k, blk=blk_at(k)) for k in range(1, n_blk)
        ]

    arrive = list(range(1, n_rep))
    if keep:
        def first_step(q, carry):
            oacc[q] = jnp.dot(backs[0], amat[q, piece_of(0), :], preferred_element_type=F32)
            return carry
        lax.fori_loop(0, n_blk, first_step, 0, unroll=4)
        for j in arrive[:-1]:
            b_copies[j].wait_recv()

            def more_step(q, carry, j=j):
                oacc[q] += jnp.dot(backs[j], amat[q, piece_of(j), :], preferred_element_type=F32)
                return carry
            lax.fori_loop(0, n_blk, more_step, 0, unroll=4)
        b_copies[arrive[-1]].wait_recv()
    else:
        for j in arrive:
            b_copies[j].wait_recv()

        def back_step(q, carry):
            prepare(q, 0)
            build(q, 0, 0, panel // CB)
            total = jnp.dot(backs[0], amat[0, piece_of(0), :], preferred_element_type=F32)
            for j in arrive:
                total = total + jnp.dot(backs[j], amat[0, piece_of(j), :], preferred_element_type=F32)
            oacc[q] = total
            return carry
        lax.fori_loop(0, n_blk, back_step, 0)

    def source_sum(k):
        q = blk_at(k)
        total = oacc[q]
        if keep:
            j = arrive[-1]
            total = total + jnp.dot(backs[j], amat[q, piece_of(j), :], preferred_element_type=F32)
        return total

    g_copies = {}
    for k in list(range(n_blk - 1, 0, -2)):
        gsend[k] = source_sum(k).astype(BF16)
        g_copies[k] = send(gsend.at[k], grecv.at[k], g_ss, g_rs, k, blk=blk_at(1))
    w2_copies = reduce_first()
    sent += w2_copies
    for k in list(range(n_blk - 2, 0, -2)):
        total = source_sum(k)
        g_copies[k + 1].wait_recv()
        gsend[k] = (total + grecv[k + 1].astype(F32)).astype(BF16)
        g_copies[k] = send(gsend.at[k], grecv.at[k], g_ss, g_rs, k, blk=blk_at(k))
    result = source_sum(0) + backs[0].astype(F32)
    sent += list(g_copies.values())
    w3_copies = reduce_second(w2_copies)
    sent += w3_copies
    for k in [1] + list(range(2, n_blk, 2)):
        g_copies[k].wait_recv()
        result = result + grecv[k].astype(F32)
    gf_ref[...] = result.T.astype(BF16)
    store(gf_ref, gf_hbm)
    for copy in w3_copies:
        copy.wait_recv()
    for q in range(n_blk):
        gw_ref[q * wch:(q + 1) * wch, :] = w3r[q]
    store(gw_ref, gw_hbm)
    for copy in sent:
        copy.wait_send()
    for copy in stored:
        copy.wait()


def write_out(*refs):
    sems = refs[-1]
    count = (len(refs) - 1) // 2
    copies = [pltpu.make_async_copy(refs[i], refs[count + i], sems.at[i]) for i in range(count)]
    for copy in copies:
        copy.start()
    for copy in copies:
        copy.wait()


def on_device(n_blk, n_rep, features, edge_rows, edge_cols, weight, bias, upstream, train_mask):
    piece, d_in = features.shape
    panel = upstream.shape[0]
    hid = weight.shape[1]
    wch = d_in // n_blk
    extra = 16 * (piece // CB)
    keep = panel * piece * n_blk * 2 <= 16 * 2**20
    sem = pltpu.SemaphoreType.DMA
    anywhere = pl.BlockSpec(memory_space=pl.ANY)
    shapes = (
        jax.ShapeDtypeStruct((piece, hid), BF16),
        jax.ShapeDtypeStruct((piece, d_in), BF16),
        jax.ShapeDtypeStruct((d_in, hid), F32),
        jax.ShapeDtypeStruct((1, hid), F32),
    )
    slots = n_blk if keep else 1
    chunks, length = edge_rows.shape[2:]
    hbm = pl.BlockSpec(memory_space=pltpu.HBM)
    results = pl.pallas_call(
        functools.partial(kernel, n_blk, n_rep, keep),
        out_shape=shapes,
        in_specs=[hbm] * 7,
        out_specs=(anywhere,) * 4,
        scratch_shapes=[
            pltpu.VMEM((piece, d_in), BF16),
            pltpu.VMEM(edge_rows.shape, jnp.int32),
            pltpu.VMEM(edge_cols.shape, jnp.int32),
            pltpu.VMEM((d_in, hid), BF16),
            pltpu.VMEM((1, hid), F32),
            pltpu.VMEM((panel // CB, CB), jnp.int32),
            pltpu.VMEM((piece, hid), BF16),
            pltpu.VMEM((piece, d_in), BF16),
            pltpu.VMEM((d_in, hid), F32),
            pltpu.VMEM((1, hid), F32),
            pltpu.VMEM((slots, chunks, CB, length), BF16),
            pltpu.VMEM((slots, chunks, CB, length), BF16),
            pltpu.VMEM((n_blk, piece, d_in), BF16),
            pltpu.VMEM((slots, panel, piece), BF16),
            pltpu.VMEM((8 if keep else panel, d_in + CB), F32),
            pltpu.VMEM((n_rep, piece + extra, d_in), BF16),
            pltpu.VMEM((n_rep, piece + extra, d_in), BF16),
            pltpu.VMEM((piece, hid), BF16),
            pltpu.VMEM((n_rep, d_in, piece), BF16),
            pltpu.VMEM((n_blk, d_in, piece), F32),
            pltpu.VMEM((n_blk, d_in, piece), BF16),
            pltpu.VMEM((n_blk, d_in, piece), BF16),
            pltpu.VMEM((n_blk, wch + 8, hid), F32),
            pltpu.VMEM((n_blk, wch + 8, hid), F32),
            pltpu.VMEM((wch + 8, hid), F32),
            pltpu.VMEM((n_rep, wch + 8, hid), F32),
            pltpu.VMEM((wch, hid), F32),
            pltpu.VMEM((n_blk, wch, hid), F32),
            sem((n_blk,)), sem((n_blk,)),
            sem((n_rep,)), sem((n_rep,)),
            sem((n_rep,)), sem((n_rep,)),
            sem((n_blk,)), sem((n_blk,)),
            sem((n_blk,)), sem((n_blk,)),
            sem((n_rep,)), sem((n_rep,)),
            sem((n_blk,)), sem((n_blk,)),
            sem((7,)),
            sem((4,)),
        ],
        compiler_params=pltpu.CompilerParams(
            collective_id=0, has_side_effects=True, vmem_limit_bytes=VMEM
        ),
    )(
        features, edge_rows, edge_cols, weight, bias.reshape(1, hid),
        train_mask.reshape(panel // CB, CB), upstream,
    )
    act, gf, gw, gb = pl.pallas_call(
        write_out,
        out_shape=shapes,
        in_specs=[anywhere] * 4,
        out_specs=(hbm,) * 4,
        scratch_shapes=[sem((4,))],
        compiler_params=pltpu.CompilerParams(vmem_limit_bytes=VMEM),
    )(*results)
    return act, gf, gw, gb.reshape(hid)


def solution(mesh):
    n_blk, n_rep = mesh.shape["blk"], mesh.shape["rep"]
    return jax.shard_map(
        functools.partial(on_device, n_blk, n_rep),
        mesh=mesh,
        in_specs=(
            P(("blk", "rep"), None),
            P("blk", None, "rep", None),
            P("blk", None, "rep", None),
            P(),
            P(),
            P("blk", None),
            P("blk"),
        ),
        out_specs=(P(("blk", "rep"), None), P(("blk", "rep"), None), P(), P()),
        check_vma=False,
    )
```

time: 52.1 us -> 49.9 us (0.958)
  local copies, waits for them, and re-layouts: 8.1 us -> 0 us
  Pallas kernels: 42.9 us -> 49.1 us
    unnamed x18 -> x0, local copies, waits for them, and re-layouts: 8.1 us -> none
    pallas_call x1 -> x2, Pallas kernels: 42.9 us -> 49.1 us  [the longest x1 38 us: on_device(): pl.pallas_call(functools.partial(kernel, n_blk, n_rep, keep), out_shape=s...]
where the time goes in v2:
time: 49.9 us; the launch traced here: 49.8 us
  Pallas kernels  49.1 us (98%)
  between operations  0.64 us (1%)
    pallas_call x1, Pallas kernels, on_device(): pl.pallas_call(functools.partial(kernel, n_blk, n_rep, keep), out_shape=s...  38 us
    pallas_call x1, Pallas kernels, on_device(): pl.pallas_call(write_out, out_shape=shapes, in_specs=[anywhere] * 4, out_...  11.1 us

profile of v2, /device:TPU:0, one launch (start us, length us, event | category | flops | bytes accessed | tf_op | source)
XLA Modules:
  0.0 49.8 jit_solution(2530392644727166929)
XLA Ops:
  0.6 38.0 %shard_map.102 = (bf16[256,256]{1,0:T(8,128)(2,1)}, bf16[256,128]{1,0:T(8,128)(2,1)}, f32[128,256]{1,0:T(8,128)}, f32[1,256]{1,0:T(1,128)}) custom-call(bf16[256,128]{1,0:T(8,128)(2,1)} %feat_hbm.1, s32[1,8,2,512]{3,2,1,0:T(2,128)} %rows_hbm.1, s32[1,8,2,512]{3,2,1,0:T(2,128)} %cols_hbm.1, bf16[128,256]{1,0:T(8,128)(2,1)} %weight_hbm.1, f32[1,256]{1,0:T(1,128)} %bitcast.4, ...), custom_call_target="tpu_custom_call" | custom-call | tf_op jit(solution)/shard_map/pallas_call | solution.py:356
  38.7 11.1 %shard_map.103 = (bf16[256,256]{1,0:T(8,128)(2,1)}, bf16[256,128]{1,0:T(8,128)(2,1)}, f32[128,256]{1,0:T(8,128)}, f32[1,256]{1,0:T(1,128)}) custom-call(bf16[256,256]{1,0:T(8,128)(2,1)} %get-tuple-element.12.refs_0_, bf16[256,128]{1,0:T(8,128)(2,1)} %get-tuple-element.13.refs_1_, f32[128,256]{1,0:T(8,128)} %get-tuple-element.14.refs_2_, ...), custom_call_target="tpu_custom_call" | custom-call | tf_op jit(solution)/shard_map/pallas_call | solution.py:407

commit v3 on v2

--- a/solution.py
+++ b/solution.py
@@ -8,7 +8,7 @@
 from jax.sharding import PartitionSpec as P
 
 CB = 128
-VMEM = 63 * 2**20
+VMEM = 48 * 2**20
 F32 = jnp.float32
 BF16 = jnp.bfloat16
 MESH = pl.DeviceIdType.MESH
@@ -36,11 +36,11 @@
 def kernel(
     n_blk, n_rep, keep,
     feat_hbm, rows_hbm, cols_hbm, weight_hbm, bias_hbm, mask_hbm, up_hbm,
-    act_hbm, gf_hbm, gw_hbm, gb_hbm,
+    act_ref, gf_ref, gw_ref, gb_ref,
     feat_ref, rows_ref, cols_ref, weight_ref, bias_ref, mask_ref,
-    act_ref, gf_ref, gw_ref, gb_ref, lowh, colh, fbuf, amat, acc, psend, precv, upbuf, backs, oacc, gsend, grecv,
+    lowh, colh, fbuf, amat, acc, psend, precv, upbuf, backs, oacc, gsend, grecv,
     w1s, w1r, w2s, w2r, w3s, w3r,
-    f_ss, f_rs, p_ss, p_rs, b_ss, b_rs, g_ss, g_rs, w1_ss, w1_rs, w2_ss, w2_rs, w3_ss, w3_rs, in_sem, out_sem,
+    f_ss, f_rs, p_ss, p_rs, b_ss, b_rs, g_ss, g_rs, w1_ss, w1_rs, w2_ss, w2_rs, w3_ss, w3_rs, in_sem,
 ):
     b = lax.axis_index("blk")
     z = lax.axis_index("rep")
@@ -83,18 +83,21 @@
     pl.semaphore_wait(barrier, n_blk + n_rep - 2)
 
     sent = []
-    stored = []
-
-    def store(src, dst):
-        copy = pltpu.make_async_copy(src, dst, out_sem.at[len(stored)])
-        copy.start()
-        stored.append(copy)
-
-    f_copies = [
-        send(feat_ref, fbuf.at[b], f_ss, f_rs, k, blk=blk_at(k))
-        for k in range(n_blk - 1, 0, -1)
-    ]
-    sent += f_copies
+    even = list(range(n_blk - 2, 0, -2))
+    f_copies = {
+        k: send(feat_ref, fbuf.at[b], f_ss, f_rs, k, blk=blk_at(k)) for k in even + [1]
+    }
+
+    def hand_on():
+        for k in even:
+            f_copies[k].wait_recv()
+            slot = fbuf.at[blk_at(k)]
+            f_copies[k + 1] = send(slot, slot, f_ss, f_rs, k + 1, blk=blk_at(1))
+
+    def all_here():
+        for k in range(1, n_blk, 2):
+            f_copies[k].wait_recv()
+
     fbuf[b] = feat_ref[...]
     for load in loads[1:3]:
         load.wait()
@@ -125,26 +128,42 @@
     def with_ones(q):
         return jnp.concatenate([fbuf[q], jnp.ones((piece, CB), BF16)], axis=1)
 
-    def pack(total, slot):
-        psend[slot, 0:piece, :] = total[:, :d_in].astype(BF16)
+    def pack(total, slot, more=None):
+        part = total[:, :d_in].astype(BF16)
+        if more is not None:
+            part = (part.astype(F32) + more[0:piece].astype(F32)).astype(BF16)
+        psend[slot, 0:piece, :] = part
         counts = total[:, d_in:]
         tall = jnp.concatenate(
             [counts[i * CB:(i + 1) * CB].T[0:16] for i in range(chunks)], axis=0
         )
+        if more is not None:
+            extra = more[piece:].astype(F32)
+            pairs = [
+                extra[16 * i:16 * i + 8] + extra[16 * i + 8:16 * i + 16] for i in range(chunks)
+            ]
+            tall = tall + jnp.concatenate([x for pair in pairs for x in (pair, pair)], axis=0)
         top = tall.astype(BF16).astype(F32)
         line = lax.broadcasted_iota(jnp.int32, tall.shape, 0)
         psend[slot, piece:, :] = jnp.where(line % 16 < 8, top, tall - top).astype(BF16)
 
-    order = ([2, 3] if n_rep == 4 else []) + [j for j in range(1, n_rep) if n_rep != 4 or j == 1]
-    p_copies = []
+    odd_rep = list(range(n_rep - 1, 1, -2))
+    even_rep = list(range(n_rep - 2, 0, -2))
+    order = even_rep + odd_rep + [1]
+    p_copies = {}
 
     def piece_of(j):
         return pl.ds(pl.multiple_of(rep_at(j) * piece, piece), piece)
 
     def push(total, j):
-        pack(total, j)
+        if j in even_rep:
+            p_copies[j + 1].wait_recv()
+            pack(total, j, precv[j + 1])
+        else:
+            pack(total, j)
         if j > 0:
-            p_copies.append(send(psend.at[j], precv.at[j], p_ss, p_rs, j, rep=rep_at(j)))
+            to = rep_at(1 if j in odd_rep else j)
+            p_copies[j] = send(psend.at[j], precv.at[j], p_ss, p_rs, j, rep=to)
 
     blank = jnp.zeros((piece, d_in + CB), F32)
     if keep:
@@ -152,28 +171,39 @@
             prepare(q, q)
             return carry
         lax.fori_loop(0, n_blk, prepare_step, 0, unroll=2)
-        lead = order[:2]
+        held = None
+        turns = odd_rep + even_rep + [1, 0]
+        lead = turns[:2]
         for j in lead:
+            if j == lead[1]:
+                hand_on()
+
             def build_step(q, carry, j=j):
                 build(q, q, rep_at(j) * chunks, chunks)
                 return carry
             lax.fori_loop(0, n_blk, build_step, 0, unroll=4)
-        for copy in f_copies:
-            copy.wait_recv()
+        all_here()
         for j in lead:
             def part_step(q, total, j=j):
                 return total + jnp.dot(
                     amat[q, piece_of(j), :], with_ones(q), preferred_element_type=F32
                 )
-            push(lax.fori_loop(0, n_blk, part_step, blank, unroll=4), j)
-        for j in order[2:] + [0]:
+            total = lax.fori_loop(0, n_blk, part_step, blank, unroll=4)
+            if j in even_rep:
+                held = (total, j)
+            else:
+                push(total, j)
+        for j in turns[2:]:
             def both_step(q, total, j=j):
                 made = build(q, q, rep_at(j) * chunks, chunks)
                 return total + jnp.dot(made, with_ones(q), preferred_element_type=F32)
             push(lax.fori_loop(0, n_blk, both_step, blank, unroll=4), j)
+            if held is not None:
+                push(*held)
+                held = None
     else:
-        for copy in f_copies:
-            copy.wait_recv()
+        hand_on()
+        all_here()
         acc[...] = jnp.zeros_like(acc)
 
         def whole_step(q, carry):
@@ -182,16 +212,16 @@
             acc[...] += jnp.dot(made, with_ones(q), preferred_element_type=F32)
             return carry
         lax.fori_loop(0, n_blk, whole_step, 0)
-        for j in order + [0]:
+        for j in odd_rep + even_rep + [1, 0]:
             push(acc[piece_of(j), :], j)
-    sent += p_copies
+    sent += list(f_copies.values()) + list(p_copies.values())
 
     gathered = psend[0, 0:piece, :].astype(F32)
     tail = psend[0, piece:, :].astype(F32)
     for load in loads[3:]:
         load.wait()
-    for copy, j in zip(p_copies, order):
-        copy.wait_recv()
+    for j in even_rep + [1]:
+        p_copies[j].wait_recv()
         gathered = gathered + precv[j, 0:piece, :].astype(F32)
         tail = tail + precv[j, piece:, :].astype(F32)
     degree_rows = [
@@ -215,7 +245,6 @@
     sent += list(b_copies.values())
 
     act_ref[...] = (pre_act * gate).astype(BF16)
-    store(act_ref, act_hbm)
     weight_part = jnp.dot(
         mixed.astype(F32).T.astype(BF16), grad_pre, preferred_element_type=F32
     )
@@ -251,12 +280,15 @@
         for q in range(1, n_rep):
             total = total + w2r[q]
         gb_ref[...] = total[wch:wch + 1]
-        store(gb_ref, gb_hbm)
         w3s[...] = total[0:wch]
         w3r[b] = total[0:wch]
-        return [
-            send(w3s, w3r.at[b], w3_ss, w3_rs, k, blk=blk_at(k)) for k in range(1, n_blk)
-        ]
+        return {k: send(w3s, w3r.at[b], w3_ss, w3_rs, k, blk=blk_at(k)) for k in even + [1]}
+
+    def hand_on_weights(copies):
+        for k in even:
+            copies[k].wait_recv()
+            slot = w3r.at[blk_at(k)]
+            copies[k + 1] = send(slot, slot, w3_ss, w3_rs, k + 1, blk=blk_at(1))
 
     arrive = list(range(1, n_rep))
     if keep:
@@ -271,8 +303,10 @@
                 oacc[q] += jnp.dot(backs[j], amat[q, piece_of(j), :], preferred_element_type=F32)
                 return carry
             lax.fori_loop(0, n_blk, more_step, 0, unroll=4)
+        w2_copies = reduce_first()
         b_copies[arrive[-1]].wait_recv()
     else:
+        w2_copies = reduce_first()
         for j in arrive:
             b_copies[j].wait_recv()
 
@@ -298,31 +332,25 @@
     for k in list(range(n_blk - 1, 0, -2)):
         gsend[k] = source_sum(k).astype(BF16)
         g_copies[k] = send(gsend.at[k], grecv.at[k], g_ss, g_rs, k, blk=blk_at(1))
-    w2_copies = reduce_first()
-    sent += w2_copies
-    for k in list(range(n_blk - 2, 0, -2)):
+    w3_copies = reduce_second(w2_copies)
+    for k in even:
         total = source_sum(k)
         g_copies[k + 1].wait_recv()
         gsend[k] = (total + grecv[k + 1].astype(F32)).astype(BF16)
         g_copies[k] = send(gsend.at[k], grecv.at[k], g_ss, g_rs, k, blk=blk_at(k))
     result = source_sum(0) + backs[0].astype(F32)
-    sent += list(g_copies.values())
-    w3_copies = reduce_second(w2_copies)
-    sent += w3_copies
+    hand_on_weights(w3_copies)
+    sent += list(g_copies.values()) + w2_copies + list(w3_copies.values())
     for k in [1] + list(range(2, n_blk, 2)):
         g_copies[k].wait_recv()
         result = result + grecv[k].astype(F32)
     gf_ref[...] = result.T.astype(BF16)
-    store(gf_ref, gf_hbm)
-    for copy in w3_copies:
-        copy.wait_recv()
+    for k in range(1, n_blk, 2):
+        w3_copies[k].wait_recv()
     for q in range(n_blk):
         gw_ref[q * wch:(q + 1) * wch, :] = w3r[q]
-    store(gw_ref, gw_hbm)
     for copy in sent:
         copy.wait_send()
-    for copy in stored:
-        copy.wait()
 
 
 def write_out(*refs):
@@ -357,7 +385,7 @@
         functools.partial(kernel, n_blk, n_rep, keep),
         out_shape=shapes,
         in_specs=[hbm] * 7,
-        out_specs=(anywhere,) * 4,
+        out_specs=(pl.BlockSpec(memory_space=pltpu.VMEM),) * 4,
         scratch_shapes=[
             pltpu.VMEM((piece, d_in), BF16),
             pltpu.VMEM(edge_rows.shape, jnp.int32),
@@ -365,10 +393,6 @@
             pltpu.VMEM((d_in, hid), BF16),
             pltpu.VMEM((1, hid), F32),
             pltpu.VMEM((panel // CB, CB), jnp.int32),
-            pltpu.VMEM((piece, hid), BF16),
-            pltpu.VMEM((piece, d_in), BF16),
-            pltpu.VMEM((d_in, hid), F32),
-            pltpu.VMEM((1, hid), F32),
             pltpu.VMEM((slots, chunks, CB, length), BF16),
             pltpu.VMEM((slots, chunks, CB, length), BF16),
             pltpu.VMEM((n_blk, piece, d_in), BF16),
@@ -395,14 +419,15 @@
             sem((n_rep,)), sem((n_rep,)),
             sem((n_blk,)), sem((n_blk,)),
             sem((7,)),
-            sem((4,)),
         ],
         compiler_params=pltpu.CompilerParams(
             collective_id=0, has_side_effects=True, vmem_limit_bytes=VMEM
         ),
     )(
-        features, edge_rows, edge_cols, weight, bias.reshape(1, hid),
-        train_mask.reshape(panel // CB, CB), upstream,
+        *[pltpu.with_memory_space_constraint(x, pltpu.HBM) for x in (
+            features, edge_rows, edge_cols, weight, bias.reshape(1, hid),
+            train_mask.reshape(panel // CB, CB), upstream,
+        )]
     )
     act, gf, gw, gb = pl.pallas_call(
         write_out,

time: 49.9 us -> 37.9 us (0.76)
  Pallas kernels: 49.1 us -> 37.1 us
    pallas_call x1, Pallas kernels: 11.1 us -> 0.76 us  [on_device(): pl.pallas_call(write_out, out_shape=shapes, in_specs=[anywhere] * 4, out_...]
    pallas_call x1, Pallas kernels: 38 us -> 36.4 us  [on_device(): pl.pallas_call(functools.partial(kernel, n_blk, n_rep, keep), out_shape=s...]
where the time goes in v3:
time: 37.9 us; the launch traced here: 37.8 us
  Pallas kernels  37.1 us (98%)
  between operations  0.64 us (2%)
    pallas_call x1, Pallas kernels, on_device(): pl.pallas_call(functools.partial(kernel, n_blk, n_rep, keep), out_shape=s...  36.4 us
    pallas_call x1, Pallas kernels, on_device(): pl.pallas_call(write_out, out_shape=shapes, in_specs=[anywhere] * 4, out_...  0.76 us

profile of v3, /device:TPU:0, one launch (start us, length us, event | category | flops | bytes accessed | tf_op | source)
XLA Modules:
  0.0 37.8 jit_solution(18356574495829947188)
XLA Ops:
  0.6 36.4 %shard_map.102 = (bf16[256,256]{1,0:T(8,128)(2,1)S(1)}, bf16[256,128]{1,0:T(8,128)(2,1)S(1)}, f32[128,256]{1,0:T(8,128)S(1)}, f32[1,256]{1,0:T(1,128)S(1)}) custom-call(bf16[256,128]{1,0:T(8,128)(2,1)} %feat_hbm.1, s32[1,8,2,512]{3,2,1,0:T(2,128)} %rows_hbm.1, s32[1,8,2,512]{3,2,1,0:T(2,128)} %cols_hbm.1, bf16[128,256]{1,0:T(8,128)(2,1)} %weight_hbm.1, ...), custom_call_target="tpu_custom_call" | custom-call | tf_op jit(solution)/shard_map/pallas_call | solution.py:384
  37.0 0.8 %shard_map.103 = (bf16[256,256]{1,0:T(8,128)(2,1)}, bf16[256,128]{1,0:T(8,128)(2,1)}, f32[128,256]{1,0:T(8,128)}, f32[1,256]{1,0:T(1,128)}) custom-call(bf16[256,256]{1,0:T(8,128)(2,1)S(1)} %get-tuple-element.12.refs_0_, bf16[256,128]{1,0:T(8,128)(2,1)S(1)} %get-tuple-element.13.refs_1_, f32[128,256]{1,0:T(8,128)S(1)} %get-tuple-element.14.refs_2_, ...), custom_call_target="tpu_custom_call" | custom-call | tf_op jit(solution)/shard_map/pallas_call | solution.py:432

commit v4 on v3

--- a/solution.py
+++ b/solution.py
@@ -38,7 +38,7 @@
     feat_hbm, rows_hbm, cols_hbm, weight_hbm, bias_hbm, mask_hbm, up_hbm,
     act_ref, gf_ref, gw_ref, gb_ref,
     feat_ref, rows_ref, cols_ref, weight_ref, bias_ref, mask_ref,
-    lowh, colh, fbuf, amat, acc, psend, precv, upbuf, backs, oacc, gsend, grecv,
+    fbuf, amat, acc, psend, precv, upbuf, backs, oacc, gsend, grecv,
     w1s, w1r, w2s, w2r, w3s, w3r,
     f_ss, f_rs, p_ss, p_rs, b_ss, b_rs, g_ss, g_rs, w1_ss, w1_rs, w2_ss, w2_rs, w3_ss, w3_rs, in_sem,
 ):
@@ -102,28 +102,24 @@
     for load in loads[1:3]:
         load.wait()
 
-    def prepare(q, slot):
-        for c in range(chunks):
-            colh[slot, c] = one_hot(cols_ref[0, q, pl.ds(c, 1), :], CB)
-            lowh[slot, c] = one_hot(rows_ref[0, q, pl.ds(c, 1), :] & (CB - 1), CB)
-
-    def build(q, slot, first, count):
-        made = []
+    def build(q, slot):
         for c in range(chunks):
             rows = rows_ref[0, q, pl.ds(c, 1), :]
-            high = jnp.broadcast_to(rows >> 7, (16, rows.shape[-1]))
-            low_hot = lowh[slot, c]
+            cols = cols_ref[0, q, pl.ds(c, 1), :]
+            wide_hot = one_hot(cols + (rows & CB), 2 * CB)
+            low_hot = one_hot(rows & (CB - 1), CB)
+            pair = jnp.broadcast_to(rows >> 8, (16, rows.shape[-1]))
             parts = []
-            for h in range(count):
-                picked = jnp.where(high == first + h, 1.0, 0.0).astype(BF16)
+            for h in range(panel // (2 * CB)):
+                picked = jnp.where(pair == h, 1.0, 0.0).astype(BF16)
                 parts.append(low_hot * jnp.concatenate([picked] * (CB // 16), axis=0))
-            made.append(lax.dot_general(
-                jnp.concatenate(parts, axis=0), colh[slot, c], NT, preferred_element_type=F32
-            ).astype(BF16))
-        at = pl.ds(pl.multiple_of(first * CB, CB), count * CB)
-        made = jnp.concatenate(made, axis=1)
-        amat[slot, at, :] = made
-        return made
+            made = lax.dot_general(
+                jnp.concatenate(parts, axis=0), wide_hot, NT, preferred_element_type=F32
+            ).astype(BF16)
+            for h in range(panel // CB):
+                amat[slot, h * CB:(h + 1) * CB, c * CB:(c + 1) * CB] = made[
+                    (h // 2) * CB:(h // 2 + 1) * CB, (h % 2) * CB:(h % 2 + 1) * CB
+                ]
 
     def with_ones(q):
         return jnp.concatenate([fbuf[q], jnp.ones((piece, CB), BF16)], axis=1)
@@ -167,49 +163,28 @@
 
     blank = jnp.zeros((piece, d_in + CB), F32)
     if keep:
-        def prepare_step(q, carry):
-            prepare(q, q)
+        def build_step(q, carry):
+            build(q, q)
             return carry
-        lax.fori_loop(0, n_blk, prepare_step, 0, unroll=2)
-        held = None
-        turns = odd_rep + even_rep + [1, 0]
-        lead = turns[:2]
-        for j in lead:
-            if j == lead[1]:
-                hand_on()
-
-            def build_step(q, carry, j=j):
-                build(q, q, rep_at(j) * chunks, chunks)
-                return carry
-            lax.fori_loop(0, n_blk, build_step, 0, unroll=4)
+        half = n_blk // 2
+        lax.fori_loop(0, half, build_step, 0, unroll=2)
+        hand_on()
+        lax.fori_loop(half, n_blk, build_step, 0, unroll=2)
         all_here()
-        for j in lead:
+        for j in odd_rep + [1] + even_rep + [0]:
             def part_step(q, total, j=j):
                 return total + jnp.dot(
                     amat[q, piece_of(j), :], with_ones(q), preferred_element_type=F32
                 )
-            total = lax.fori_loop(0, n_blk, part_step, blank, unroll=4)
-            if j in even_rep:
-                held = (total, j)
-            else:
-                push(total, j)
-        for j in turns[2:]:
-            def both_step(q, total, j=j):
-                made = build(q, q, rep_at(j) * chunks, chunks)
-                return total + jnp.dot(made, with_ones(q), preferred_element_type=F32)
-            push(lax.fori_loop(0, n_blk, both_step, blank, unroll=4), j)
-            if held is not None:
-                push(*held)
-                held = None
+            push(lax.fori_loop(0, n_blk, part_step, blank, unroll=4), j)
     else:
         hand_on()
         all_here()
         acc[...] = jnp.zeros_like(acc)
 
         def whole_step(q, carry):
-            prepare(q, 0)
-            made = build(q, 0, 0, panel // CB)
-            acc[...] += jnp.dot(made, with_ones(q), preferred_element_type=F32)
+            build(q, 0)
+            acc[...] += jnp.dot(amat[0], with_ones(q), preferred_element_type=F32)
             return carry
         lax.fori_loop(0, n_blk, whole_step, 0)
         for j in odd_rep + even_rep + [1, 0]:
@@ -311,8 +286,7 @@
             b_copies[j].wait_recv()
 
         def back_step(q, carry):
-            prepare(q, 0)
-            build(q, 0, 0, panel // CB)
+            build(q, 0)
             total = jnp.dot(backs[0], amat[0, piece_of(0), :], preferred_element_type=F32)
             for j in arrive:
                 total = total + jnp.dot(backs[j], amat[0, piece_of(j), :], preferred_element_type=F32)
@@ -379,7 +353,6 @@
         jax.ShapeDtypeStruct((1, hid), F32),
     )
     slots = n_blk if keep else 1
-    chunks, length = edge_rows.shape[2:]
     hbm = pl.BlockSpec(memory_space=pltpu.HBM)
     results = pl.pallas_call(
         functools.partial(kernel, n_blk, n_rep, keep),
@@ -393,8 +366,6 @@
             pltpu.VMEM((d_in, hid), BF16),
             pltpu.VMEM((1, hid), F32),
             pltpu.VMEM((panel // CB, CB), jnp.int32),
-            pltpu.VMEM((slots, chunks, CB, length), BF16),
-            pltpu.VMEM((slots, chunks, CB, length), BF16),
             pltpu.VMEM((n_blk, piece, d_in), BF16),
             pltpu.VMEM((slots, panel, piece), BF16),
             pltpu.VMEM((8 if keep else panel, d_in + CB), F32),

time: 37.9 us -> 37.9 us (level)
  no operation moved by 1% of the time
where the time goes in v4:
time: 37.9 us; the launch traced here: 37.8 us
  Pallas kernels  37.1 us (98%)
  between operations  0.64 us (2%)
    pallas_call x1, Pallas kernels, on_device(): pl.pallas_call(functools.partial(kernel, n_blk, n_rep, keep), out_shape=s...  36.4 us
    pallas_call x1, Pallas kernels, on_device(): pl.pallas_call(write_out, out_shape=shapes, in_specs=[anywhere] * 4, out_...  0.76 us

profile of v4, /device:TPU:0, one launch (start us, length us, event | category | flops | bytes accessed | tf_op | source)
XLA Modules:
  0.0 37.8 jit_solution(583934805059583989)
XLA Ops:
  0.6 36.4 %shard_map.102 = (bf16[256,256]{1,0:T(8,128)(2,1)S(1)}, bf16[256,128]{1,0:T(8,128)(2,1)S(1)}, f32[128,256]{1,0:T(8,128)S(1)}, f32[1,256]{1,0:T(1,128)S(1)}) custom-call(bf16[256,128]{1,0:T(8,128)(2,1)} %feat_hbm.1, s32[1,8,2,512]{3,2,1,0:T(2,128)} %rows_hbm.1, s32[1,8,2,512]{3,2,1,0:T(2,128)} %cols_hbm.1, bf16[128,256]{1,0:T(8,128)(2,1)} %weight_hbm.1, ...), custom_call_target="tpu_custom_call" | custom-call | tf_op jit(solution)/shard_map/pallas_call | solution.py:357
  37.0 0.8 %shard_map.103 = (bf16[256,256]{1,0:T(8,128)(2,1)}, bf16[256,128]{1,0:T(8,128)(2,1)}, f32[128,256]{1,0:T(8,128)}, f32[1,256]{1,0:T(1,128)}) custom-call(bf16[256,256]{1,0:T(8,128)(2,1)S(1)} %get-tuple-element.12.refs_0_, bf16[256,128]{1,0:T(8,128)(2,1)S(1)} %get-tuple-element.13.refs_1_, f32[128,256]{1,0:T(8,128)S(1)} %get-tuple-element.14.refs_2_, ...), custom_call_target="tpu_custom_call" | custom-call | tf_op jit(solution)/shard_map/pallas_call | solution.py:403
